TPU v7x, 256 devices: a whole 4x4x8 slice. The times are simulated.
256 devices in a mesh: row: 16 (over y, z_lo), col: 16 (over x, z_hi, core).
Axes of the slice: x: 4, y: 4, z: 8 (z_hi: 2, z_lo: 4; z = z_hi * 4 + z_lo), core: 2. Of those that a mesh axis runs over, the one named last changes fastest.
Arguments:
- activations: bfloat16 [2048, 28672], P('col', 'row'), may hold values from -36 to 36
- output_gradient: bfloat16 [2048, 8192], P('row', 'col'), may hold values from -6 to 6
- frozen_weight: bfloat16 [28672, 8192], P('row', 'col'), may hold values from -0.0390625 to 0.0390625
- sparsity_mask_pattern: int32 [7168, 8192], P('row', 'col'), may hold values from 0 to 5
- adapter_left_factor: bfloat16 [28672, 16], P('row'), may hold values from -0.19921875 to 0.19921875
- adapter_right_factor: bfloat16 [16, 8192], P(None, 'col'), may hold values from -0.359375 to 0.359375
Outputs:
- input_grad: bfloat16 [2048, 28672], P('col', 'row')
- left_grad: float32 [28672, 16], P('row')
- right_grad: float32 [16, 8192], P(None, 'col')
Inputs may be any that keep to these rules, and one draw needn't show every extreme that they name: `sparsity_mask_pattern`: a pattern number of the 2:4 mask.
All inputs are finite; a program needn't handle non-finite values.
Results may differ from a plain program's by a relative error of at most 0.005.
Values may be sent and summed in bfloat16 or wider, within the bound.
A program may use at most 64 MiB of HBM per device.

v0:
```python
import jax
import jax.numpy as jnp
from jax import lax
from jax.sharding import PartitionSpec as P

PAIRS = ((0, 1), (0, 2), (0, 3), (1, 2), (1, 3), (2, 3))
ADAPTER_SCALE = 2.0


def expand_mask(code):
    groups = []
    for column in range(4):
        kept = jnp.zeros(code.shape, jnp.float32)
        for pattern in range(6):
            if column in PAIRS[pattern]:
                kept = kept + (code == pattern).astype(jnp.float32)
        groups.append(kept)
    stacked = jnp.stack(groups, axis=1)
    return stacked.reshape(code.shape[0] * 4, code.shape[1])


def input_sums_of(grad_rows, merged):
    return lax.psum_scatter(
        lax.dot_general(
            grad_rows, merged, (((1,), (1,)), ((), ())), preferred_element_type=jnp.float32
        ),
        "col",
        scatter_dimension=0,
        tiled=True,
    )


def weight_grad_of(activations, grad_rows):
    return lax.dot_general(
        lax.all_gather(activations, "col", axis=0, tiled=True),
        grad_rows,
        (((0,), (0,)), ((), ())),
        preferred_element_type=jnp.float32,
    )


def per_device(
    activations,
    output_gradient,
    frozen_weight,
    sparsity_mask_pattern,
    adapter_left_factor,
    adapter_right_factor,
):
    masked = expand_mask(sparsity_mask_pattern)
    low_rank_update = jnp.dot(
        adapter_left_factor, adapter_right_factor, preferred_element_type=jnp.float32
    )
    merged = (
        masked * (frozen_weight.astype(jnp.float32) + ADAPTER_SCALE * low_rank_update)
    ).astype(jnp.bfloat16)
    grad_rows = lax.all_gather(output_gradient, "row", axis=0, tiled=True)
    all_tokens = grad_rows.shape[0]
    input_sums = input_sums_of(grad_rows, merged)
    held, later_rows = lax.optimization_barrier((input_sums, activations))
    weight_grad = weight_grad_of(later_rows, grad_rows)
    input_grad = held.astype(jnp.bfloat16)
    pruned_gradient = (masked * weight_grad / all_tokens).astype(jnp.bfloat16)
    left_partial = ADAPTER_SCALE * lax.dot_general(
        pruned_gradient,
        adapter_right_factor,
        (((1,), (1,)), ((), ())),
        preferred_element_type=jnp.float32,
    )
    right_partial = ADAPTER_SCALE * lax.dot_general(
        adapter_left_factor,
        pruned_gradient,
        (((0,), (0,)), ((), ())),
        preferred_element_type=jnp.float32,
    )
    right_grad = lax.psum(right_partial, "row")
    left_grad = lax.psum(left_partial, "col")
    return (input_grad, left_grad, right_grad)


def solution(mesh):
    in_specs = (
        P("col", "row"),
        P("row", "col"),
        P("row", "col"),
        P("row", "col"),
        P("row", None),
        P(None, "col"),
    )
    out_specs = (P("col", "row"), P("row", None), P(None, "col"))
    return jax.shard_map(
        per_device, mesh=mesh, in_specs=in_specs, out_specs=out_specs, check_vma=False
    )
```

profile of v0, /device:TPU:8, one launch (start us, length us, event | category | flops | bytes accessed | tf_op | source)
XLA Modules:
  0.0 587.4 jit_solution(565895379995326784)
XLA Ops:
  7.2 0.0 copy-start
  7.2 0.0 copy-start.1
  7.2 0.0 all-gather.3.cloned.1.call-start
  7.2 0.7 all-gather.3.cloned.1.call-update
  7.9 0.0 reduce-scatter.2.cloned.1.call-start
  8.0 1.7 fusion.1
  9.7 1.6 fusion.2
  11.3 0.0 copy-done.1
  11.3 0.3 fusion.3
  11.6 0.2 fusion.4
  11.9 0.4 pad_maximum_fusion
  12.2 4.2 copy.9
  16.4 5.2 reshape.9
  21.7 71.8 %all-gather.3.cloned.1.call-done = bf16[2048,512]{1,0:T(8,128)(2,1)} async-done(((bf16[128,512]{1,0:T(8,128)(2,1)}), bf16[2048,512]{1,0:T(8,128)(2,1)}) %all-gather.3.cloned.1.call-update) | async-done | bytes 2097168 | tf_op jit(solution)/shard_map/all_gather | solution.py:57
  93.5 0.0 copy-done
  93.5 0.0 copy-done.2
  93.5 9.9 %convolution_bitcast_fusion = f32[2048,1792]{0,1:T(8,128)} fusion(bf16[2048,512]{1,0:T(8,128)(2,1)} %all-gather.3.cloned.1.call-done, f32[1792,512]{1,0:T(8,128)} %reshape.9, bf16[1792,512]{1,0:T(8,128)(2,1)S(1)} %copy-done.3, bf16[1792,16]{0,1:T(8,128)(2,1)S(1)} %copy-done, bf16[16,512]{1,0:T(8,128)(2,1)S(1)} %copy-done.2), kind=kOutput, calls=%fused_computation | convolution fusion | flops 3792044032 | bytes 22355968 | tf_op jit(solution)/shard_map/dot_general | solution.py:24
  103.4 0.0 reduce-scatter.2.cloned.1.call-update
  103.4 0.0 all-gather.5.cloned.1.call-start
  103.5 200.1 %reduce-scatter.2.cloned.1.call-done = f32[128,1792]{0,1:T(8,128)} async-done(((f32[2048,1792]{0,1:T(8,128)}), f32[128,1792]{0,1:T(8,128)}) %reduce-scatter.2.cloned.1.call-update) | async-done | bytes 917520 | tf_op jit(solution)/shard_map/reduce_scatter | solution.py:23
  303.6 0.0 all-gather.5.cloned.1.call-update
  303.6 0.0 all-reduce.2.cloned.1.call-start
  303.7 1.2 convert_element_type.44
  304.9 1.0 copy.10
  305.9 96.1 %all-gather.5.cloned.1.call-done = bf16[2048,1792]{1,0:T(8,128)(2,1)} async-done(((bf16[128,1792]{1,0:T(8,128)(2,1)}), bf16[2048,1792]{1,0:T(8,128)(2,1)}) %all-gather.5.cloned.1.call-update) | async-done | bytes 7340048 | tf_op jit(solution)/shard_map/all_gather | solution.py:35
  402.0 8.8 %multiply_convert_fusion = bf16[1792,512]{1,0:T(8,128)(2,1)S(1)} fusion(f32[1792,512]{1,0:T(8,128)} %reshape.9, bf16[2048,1792]{1,0:T(8,128)(2,1)} %all-gather.5.cloned.1.call-done, bf16[2048,512]{1,0:T(8,128)(2,1)} %all-gather.3.cloned.1.call-done), kind=kOutput, calls=%fused_computation.2 | convolution fusion | flops 3760848896 | bytes 14942208 | tf_op jit(solution)/shard_map/dot_general | solution.py:34
  410.7 1.2 convolution_multiply_fusion
  412.0 0.0 all-reduce.2.cloned.1.call-update
  412.0 0.3 fusion
  412.3 68.6 %psum.15 = f32[16,512]{1,0:T(8,128)} all-reduce(f32[16,512]{1,0:T(8,128)S(1)} %fusion), channel_id=1, replica_groups=mesh['row'=16,'col'=16] {'row'}, use_global_device_ids=true, to_apply=%region_2.0 | all-reduce | flops 8192 | bytes 65536 | tf_op jit(solution)/shard_map/psum | solution.py:76
  480.9 98.4 %all-reduce.2.cloned.1.call-done = f32[1792,16]{0,1:T(8,128)} async-done(((f32[1792,16]{0,1:T(8,128)}), f32[1792,16]{0,1:T(8,128)}) %all-reduce.2.cloned.1.call-update) | async-done | bytes 114704 | tf_op jit(solution)/shard_map/psum | solution.py:77
  579.3 1.6 copy.12
  (3 shorter events, 0.0 us)
Async XLA Ops:
  7.2 86.3 %copy-start = (bf16[1792,16]{0,1:T(8,128)(2,1)S(1)}, bf16[1792,16]{0,1:T(8,128)(2,1)}, u32[]{:S(2)}) copy-start(bf16[1792,16]{0,1:T(8,128)(2,1)} %param.10) | copy-start | bytes 172036
  7.2 4.1 copy-start.1
  7.2 86.3 %all-gather.3.cloned.1.call-start = ((), (), s32[]{:S(2)}) async-start(), calls=%async_computation.1 | async-start | bytes 2228224 | tf_op jit(solution)/shard_map/all_gather | solution.py:57
  7.9 295.7 %reduce-scatter.2.cloned.1.call-start = ((), (), s32[]{:S(2)}) async-start(), calls=%async_computation.2 | async-start | bytes 15597568 | tf_op jit(solution)/shard_map/reduce_scatter | solution.py:23
  16.4 77.0 %copy-start.2 = (bf16[16,512]{1,0:T(8,128)(2,1)S(1)}, bf16[16,512]{1,0:T(8,128)(2,1)}, u32[]{:S(2)}) copy-start(bf16[16,512]{1,0:T(8,128)(2,1)} %param.11) | copy-start | bytes 49156
  16.4 77.1 %copy-start.3 = (bf16[1792,512]{1,0:T(8,128)(2,1)S(1)}, bf16[1792,512]{1,0:T(8,128)(2,1)}, u32[]{:S(2)}) copy-start(bf16[1792,512]{1,0:T(8,128)(2,1)} %param.8) | copy-start | bytes 5505028
  103.4 298.5 %all-gather.5.cloned.1.call-start = ((), (), s32[]{:S(2)}) async-start(), calls=%async_computation.3 | async-start | bytes 7798784 | tf_op jit(solution)/shard_map/all_gather | solution.py:35
  303.6 275.7 %all-reduce.2.cloned.1.call-start = ((), (), s32[]{:S(2)}) async-start(), calls=%async_computation.4 | async-start | bytes 229376 | tf_op jit(solution)/shard_map/psum | solution.py:77
Sparse Core Ops, SparseCore 0:
  9.8 83.5 all-gather.2
  103.5 200.0 reduce-scatter.1
  306.7 95.2 all-gather.4
  412.1 167.1 all-reduce.1
where the time goes:
time: 588 us; the launch traced here: 587 us
  waiting for transfers between devices  467 us (79%)
  blocking collectives  68.6 us (12%)
  matrix products  20.3 us (3%)
  between operations  13.8 us (2%)
  local copies, waits for them, and re-layouts  12 us (2%)
    reduce_scatter x1, waiting for transfers between devices, input_sums_of(): lax.psum_scatter(lax.dot_general(grad_rows, merged, (((1,), (1,)), ((), (...  200 us
    psum x1, waiting for transfers between devices, per_device(): left_grad = lax.psum(left_partial, 'col')  98.4 us
    all_gather x1, waiting for transfers between devices, weight_grad_of(): lax.all_gather(activations, 'col', axis=0, tiled=True)  96.1 us
    all_gather x1, waiting for transfers between devices, per_device(): grad_rows = lax.all_gather(output_gradient, 'row', axis=0, tiled=True)  71.8 us
    psum x1, blocking collectives, per_device(): right_grad = lax.psum(right_partial, 'row')  68.6 us
  transfers between devices with their start and end apart: 4, of which 4 were waited for; matrix products, arithmetic and copies ran while one was open for 3% of the time, Pallas kernels for 0%

commit v1 on v0

--- a/solution.py
+++ b/solution.py
@@ -54,7 +54,9 @@
     merged = (
         masked * (frozen_weight.astype(jnp.float32) + ADAPTER_SCALE * low_rank_update)
     ).astype(jnp.bfloat16)
-    grad_rows = lax.all_gather(output_gradient, "row", axis=0, tiled=True)
+    grad_rows = jnp.concatenate(
+        lax.all_to_all(jnp.stack([output_gradient] * lax.axis_size("row")), "row", 0, 0), axis=0
+    )
     all_tokens = grad_rows.shape[0]
     input_sums = input_sums_of(grad_rows, merged)
     held, later_rows = lax.optimization_barrier((input_sums, activations))

time: 588 us -> 556 us (0.946)
  waiting for transfers between devices: 467 us -> 426 us
  starting transfers between devices: 0.16 us -> 9.11 us
    all_gather x1 -> x0, waiting for transfers between devices: 71.8 us -> none  [per_device(): grad_rows = lax.all_gather(output_gradient, 'row', axis=0, tiled=True)]
    all_to_all x0 -> x1, waiting for transfers between devices: none -> 36.5 us  [per_device(): lax.all_to_all(jnp.stack([output_gradient] * lax.axis_size('row')), 'row'...]
    all_to_all x0 -> x1, starting transfers between devices: none -> 8.99 us  [per_device(): lax.all_to_all(jnp.stack([output_gradient] * lax.axis_size('row')), 'row'...]
  transfers between devices with their start and end apart: 4 -> 4, of which waited for: 4 -> 4; matrix products, arithmetic and copies ran while one was open for 3% -> 2% of each run, Pallas kernels for 0% -> 0%
where the time goes in v1:
time: 556 us; the launch traced here: 555 us
  waiting for transfers between devices  426 us (77%)
  blocking collectives  68.6 us (12%)
  matrix products  20.6 us (4%)
  local copies, waits for them, and re-layouts  14.4 us (3%)
  between operations  13.8 us (2%)
  starting transfers between devices  9.11 us (2%)
    reduce_scatter x1, waiting for transfers between devices, input_sums_of(): lax.psum_scatter(lax.dot_general(grad_rows, merged, (((1,), (1,)), ((), (...  195 us
    psum x1, waiting for transfers between devices, per_device(): left_grad = lax.psum(left_partial, 'col')  98.4 us
    all_gather x1, waiting for transfers between devices, weight_grad_of(): lax.all_gather(activations, 'col', axis=0, tiled=True)  96.2 us
    psum x1, blocking collectives, per_device(): right_grad = lax.psum(right_partial, 'row')  68.6 us
    all_to_all x1, waiting for transfers between devices, per_device(): lax.all_to_all(jnp.stack([output_gradient] * lax.axis_size('row')), 'row'...  36.5 us
  transfers between devices with their start and end apart: 4, of which 4 were waited for; matrix products, arithmetic and copies ran while one was open for 2% of the time, Pallas kernels for 0%

profile of v1, /device:TPU:8, one launch (start us, length us, event | category | flops | bytes accessed | tf_op | source)
XLA Modules:
  0.0 555.4 jit_solution(8662033807720980948)
XLA Ops:
  7.2 0.0 copy-start
  7.2 0.0 copy-start.1
  7.2 2.5 stack.17
  9.7 9.0 %all-to-all-start = ((bf16[16,128,512]{2,1,0:T(8,128)(2,1)}), bf16[16,128,512]{2,1,0:T(8,128)(2,1)S(1)}, u32[]{:S(2)}, u32[]{:S(2)}) async-start(bf16[16,128,512]{2,1,0:T(8,128)(2,1)} %stack.17), calls=%async_computation | async-start | bytes 4194304 | tf_op jit(solution)/shard_map/all_to_all | solution.py:58
  18.7 0.0 reduce-scatter.2.cloned.1.call-start
  18.8 0.0 copy-done.1
  18.8 0.5 fusion.1
  19.3 0.4 fusion.2
  19.7 0.3 fusion.3
  20.0 0.2 fusion.4
  20.3 0.4 pad_maximum_fusion
  20.7 4.2 copy.9
  24.8 5.1 reshape.14
  30.0 36.5 %all-to-all-done = bf16[16,128,512]{2,1,0:T(8,128)(2,1)S(1)} async-done(((bf16[16,128,512]{2,1,0:T(8,128)(2,1)}), bf16[16,128,512]{2,1,0:T(8,128)(2,1)S(1)}, u32[]{:S(2)}, u32[]{:S(2)}) %all-to-all-start) | async-done | bytes 2097184 | tf_op jit(solution)/shard_map/all_to_all | solution.py:58
  66.4 0.0 copy-done
  66.4 0.0 copy-done.3
  66.4 10.2 %convolution_bitcast_fusion = f32[2048,1792]{0,1:T(8,128)} fusion(bf16[2048,512]{1,0:T(8,128)(2,1)S(1)} %bitcast.22, f32[1792,512]{1,0:T(8,128)} %reshape.14, bf16[1792,512]{1,0:T(8,128)(2,1)} %param.8, bf16[1792,16]{0,1:T(8,128)(2,1)S(1)} %copy-done, bf16[16,512]{1,0:T(8,128)(2,1)S(1)} %copy-done.3), kind=kOutput, calls=%fused_computation | convolution fusion | flops 3792044032 | bytes 22355968 | tf_op jit(solution)/shard_map/dot_general | solution.py:24
  76.7 0.0 reduce-scatter.2.cloned.1.call-update
  76.7 0.0 all-gather.2.cloned.1.call-start
  76.8 194.8 %reduce-scatter.2.cloned.1.call-done = f32[128,1792]{0,1:T(8,128)} async-done(((f32[2048,1792]{0,1:T(8,128)}), f32[128,1792]{0,1:T(8,128)}) %reduce-scatter.2.cloned.1.call-update) | async-done | bytes 917520 | tf_op jit(solution)/shard_map/reduce_scatter | solution.py:23
  271.5 0.0 all-gather.2.cloned.1.call-update
  271.6 0.0 all-reduce.2.cloned.1.call-start
  271.6 1.2 convert_element_type.44
  272.8 1.0 copy.10
  273.8 96.2 %all-gather.2.cloned.1.call-done = bf16[2048,1792]{1,0:T(8,128)(2,1)} async-done(((bf16[128,1792]{1,0:T(8,128)(2,1)}), bf16[2048,1792]{1,0:T(8,128)(2,1)}) %all-gather.2.cloned.1.call-update) | async-done | bytes 7340048 | tf_op jit(solution)/shard_map/all_gather | solution.py:35
  370.0 8.8 %multiply_convert_fusion = bf16[1792,512]{1,0:T(8,128)(2,1)S(1)} fusion(f32[1792,512]{1,0:T(8,128)} %reshape.14, bf16[2048,1792]{1,0:T(8,128)(2,1)} %all-gather.2.cloned.1.call-done, bf16[2048,512]{1,0:T(8,128)(2,1)} %bitcast.23), kind=kOutput, calls=%fused_computation.2 | convolution fusion | flops 3760848896 | bytes 14942208 | tf_op jit(solution)/shard_map/dot_general | solution.py:34
  378.8 1.2 convolution_multiply_fusion
  380.0 0.0 all-reduce.2.cloned.1.call-update
  380.0 0.3 fusion
  380.4 68.6 %psum.15 = f32[16,512]{1,0:T(8,128)} all-reduce(f32[16,512]{1,0:T(8,128)S(1)} %fusion), channel_id=1, replica_groups=mesh['row'=16,'col'=16] {'row'}, use_global_device_ids=true, to_apply=%region_2.0 | all-reduce | flops 8192 | bytes 65536 | tf_op jit(solution)/shard_map/psum | solution.py:78
  449.0 98.4 %all-reduce.2.cloned.1.call-done = f32[1792,16]{0,1:T(8,128)} async-done(((f32[1792,16]{0,1:T(8,128)}), f32[1792,16]{0,1:T(8,128)}) %all-reduce.2.cloned.1.call-update) | async-done | bytes 114704 | tf_op jit(solution)/shard_map/psum | solution.py:79
  547.3 1.6 copy.12
  (3 shorter events, 0.0 us)
Async XLA Ops:
  7.2 59.3 %copy-start = (bf16[1792,16]{0,1:T(8,128)(2,1)S(1)}, bf16[1792,16]{0,1:T(8,128)(2,1)}, u32[]{:S(2)}) copy-start(bf16[1792,16]{0,1:T(8,128)(2,1)} %param.10) | copy-start | bytes 172036
  7.2 11.6 %copy-start.1 = (s32[448,512]{1,0:T(8,128)S(1)}, s32[448,512]{1,0:T(8,128)}, u32[]{:S(2)}) copy-start(s32[448,512]{1,0:T(8,128)} %param.9) | copy-start | bytes 2752516
  9.7 56.7 %all-to-all-start = ((bf16[16,128,512]{2,1,0:T(8,128)(2,1)}), bf16[16,128,512]{2,1,0:T(8,128)(2,1)S(1)}, u32[]{:S(2)}, u32[]{:S(2)}) async-start(bf16[16,128,512]{2,1,0:T(8,128)(2,1)} %stack.17), calls=%async_computation | async-start | bytes 4194304 | tf_op jit(solution)/shard_map/all_to_all | solution.py:58
  18.7 252.8 %reduce-scatter.2.cloned.1.call-start = ((), (), s32[]{:S(2)}) async-start(), calls=%async_computation.2 | async-start | bytes 15597568 | tf_op jit(solution)/shard_map/reduce_scatter | solution.py:23
  24.8 41.6 %copy-start.3 = (bf16[16,512]{1,0:T(8,128)(2,1)S(1)}, bf16[16,512]{1,0:T(8,128)(2,1)}, u32[]{:S(2)}) copy-start(bf16[16,512]{1,0:T(8,128)(2,1)} %param.11) | copy-start | bytes 49156
  66.4 10.3 %copy-start.2 = (bf16[16,128,512]{2,1,0:T(8,128)(2,1)}, bf16[16,128,512]{2,1,0:T(8,128)(2,1)S(1)}, u32[]{:S(2)}) copy-start(bf16[16,128,512]{2,1,0:T(8,128)(2,1)S(1)} %all-to-all-done) | copy-start | bytes 6291460
  76.7 293.3 %all-gather.2.cloned.1.call-start = ((), (), s32[]{:S(2)}) async-start(), calls=%async_computation.3 | async-start | bytes 7798784 | tf_op jit(solution)/shard_map/all_gather | solution.py:35
  271.6 275.8 %all-reduce.2.cloned.1.call-start = ((), (), s32[]{:S(2)}) async-start(), calls=%async_computation.4 | async-start | bytes 229376 | tf_op jit(solution)/shard_map/psum | solution.py:79
Sparse Core Ops, SparseCore 0:
  76.8 194.6 reduce-scatter.1
  274.6 95.3 all-gather.1
  380.2 167.1 all-reduce.1
